TPU v7x, 32 devices: a whole 2x2x4 slice. The times are simulated.
32 devices in a mesh: expert: 16 (over z, y, x), tensor: 2 (over core).
Axes of the slice: x: 2, y: 2, z: 4, core: 2. Of those that a mesh axis runs over, the one named last changes fastest.
Arguments:
- tokens: bfloat16 [512, 7168], P('expert', 'tensor'), may hold values from -6 to 6
- expert_ids: int32 [512, 8], P('expert'), may hold values from 0 to 15, all different within a row; in each aligned block of 32 rows (0 to 31, 32 to 63, ...) at most 32 rows name the same one
- combine: float32 [512, 8], P('expert'), may hold values from 0.1 to 0.5
- w_in: bfloat16 [16, 7168, 2048], P('expert', None, 'tensor'), may hold values from -0.0625 to 0.0625
- w_down: bfloat16 [16, 1024, 7168], P('expert', None, 'tensor'), may hold values from -0.1875 to 0.1875
Outputs:
- moe_out: bfloat16 [512, 7168], P('expert', 'tensor')
Inputs may be any that keep to these rules, and one draw needn't show every extreme that they name: `expert_ids`: each row names 8 different experts. Within the 32 tokens of one index of expert, no expert is named by more than 32 rows.
All inputs are finite; a program needn't handle non-finite values.
Results may differ from a plain program's by a relative error of at most 0.008.
Values may be sent and summed in bfloat16 or wider, within the bound.
A program may use at most 64 MiB of HBM per device.

v0:
```python
import jax
import jax.numpy as jnp
from jax import lax
from jax.sharding import PartitionSpec as P

TOP = 8


def route_slots(expert_ids, experts):
    one_hot = (
        expert_ids[:, :, None] == jnp.arange(experts, dtype=jnp.int32)[None, None, :]
    ).astype(jnp.int32)
    per_token = jnp.sum(one_hot, axis=1)
    before = jnp.cumsum(per_token, axis=0) - per_token
    return jnp.take_along_axis(before, expert_ids, axis=1)


def per_device(tokens, expert_ids, combine, w_in, w_down):
    experts = lax.axis_size("expert")
    tok_group = tokens.shape[0]
    capacity = min(tok_group, 3 * tok_group * TOP // experts)
    slot_index = route_slots(expert_ids, experts)
    target = (expert_ids * capacity + slot_index).reshape(-1)
    w_local = w_in[0]
    down_local = w_down[0]
    feat_width = tokens.shape[1]
    spread = jnp.repeat(tokens, TOP, axis=0)
    buffer = jnp.zeros((experts * capacity, feat_width), tokens.dtype).at[target].set(spread)
    arrived = lax.all_to_all(
        buffer.reshape(experts, capacity, feat_width),
        "expert",
        split_axis=0,
        concat_axis=0,
        tiled=True,
    )
    token_rows = arrived.reshape(experts * capacity, tokens.shape[1])
    weights = w_local
    gate_up = jnp.dot(
        lax.all_gather(token_rows, "tensor", axis=1, tiled=True),
        weights,
        preferred_element_type=jnp.float32,
    )
    half_width = w_local.shape[1] // 2
    hidden = (jax.nn.silu(gate_up[:, :half_width]) * gate_up[:, half_width:]).astype(jnp.bfloat16)
    weights = down_local
    expert_out = jnp.dot(
        lax.all_gather(hidden, "tensor", axis=1, tiled=True),
        weights,
        preferred_element_type=jnp.float32,
    ).astype(jnp.bfloat16)
    returned = lax.all_to_all(
        expert_out.reshape(experts, capacity, down_local.shape[1]),
        "expert",
        split_axis=0,
        concat_axis=0,
        tiled=True,
    )
    returned_flat = returned.reshape(experts * capacity, down_local.shape[1])
    picked = returned_flat[target].reshape(tok_group, TOP, down_local.shape[1])
    combined = jnp.einsum("tk,tkd->td", combine, picked.astype(jnp.float32))
    return combined.astype(jnp.bfloat16)


def solution(mesh):
    in_specs = (
        P("expert", "tensor"),
        P("expert", None),
        P("expert", None),
        P("expert", None, "tensor"),
        P("expert", None, "tensor"),
    )
    out_specs = P("expert", "tensor")
    return jax.shard_map(
        per_device, mesh=mesh, in_specs=in_specs, out_specs=out_specs, check_vma=False
    )
```

profile of v0, /device:TPU:14, one launch (start us, length us, event | category | flops | bytes accessed | tf_op | source)
XLA Modules:
  0.0 261.7 jit_solution(5708212414219950984)
XLA Ops:
  6.5 0.0 copy-start
  6.5 0.0 all-gather.3.cloned.1.call-start
  6.5 0.7 convert_reduce_fusion
  7.3 0.8 copy.12
  8.1 0.1 copy.16
  8.1 0.1 reduce_window_sum.11
  8.2 0.1 reshape.75
  8.3 1.9 gather_fusion.1
  10.2 0.1 reshape.78
  10.3 0.1 reshape.60
  10.5 0.0 copy-done
  10.5 5.4 %scatter_custom_fusion = bf16[512,3584]{1,0:T(8,128)(2,1)} fusion(s32[256]{0:T(256)S(1)} %bitcast.34, bf16[]{:T(256)} %constant.10.clone.1, bf16[32,3584]{1,0:T(8,128)(2,1)S(1)} %copy-done), kind=kCustom, calls=%fused_computation.10 | custom fusion | bytes 3899394 | tf_op jit(solution)/shard_map/scatter | solution.py:28
  15.9 87.7 %all_to_all.10 = bf16[16,32,3584]{2,1,0:T(8,128)(2,1)} all-to-all(bf16[16,32,3584]{2,1,0:T(8,128)(2,1)} %bitcast.31), channel_id=1, replica_groups=mesh['expert'=16,'tensor'=2] {'expert'}, dimensions={0} | all-to-all | bytes 7340032 | tf_op jit(solution)/shard_map/all_to_all | solution.py:29
  103.6 0.0 all-gather.3.cloned.1.call-update
  103.6 0.0 all-gather.5.cloned.1.call-start
  103.6 18.6 %all-gather.3.cloned.1.call-done = bf16[512,7168]{1,0:T(8,128)(2,1)} async-done(((bf16[512,3584]{1,0:T(8,128)(2,1)}), bf16[512,7168]{1,0:T(8,128)(2,1)}) %all-gather.3.cloned.1.call-update) | async-done | bytes 7340048 | tf_op jit(solution)/shard_map/all_gather | solution.py:39
  122.3 13.1 %fusion = f32[512,1024]{1,0:T(8,128)S(1)} fusion(bf16[512,7168]{1,0:T(8,128)(2,1)} %all-gather.3.cloned.1.call-done, bf16[1,7168,1024]{2,1,0:T(8,128)(2,1)} %param.8), kind=kOutput, calls=%fused_computation.3 | convolution fusion | flops 7516192768 | bytes 24117248 | tf_op jit(solution)/shard_map/dot_general | solution.py:38
  135.4 1.1 fusion.12
  136.5 0.0 all-gather.5.cloned.1.call-update
  136.5 10.4 %all-gather.5.cloned.1.call-done = bf16[512,1024]{1,0:T(8,128)(2,1)} async-done(((bf16[512,512]{1,0:T(8,128)(2,1)}), bf16[512,1024]{1,0:T(8,128)(2,1)}) %all-gather.5.cloned.1.call-update) | async-done | bytes 1048592 | tf_op jit(solution)/shard_map/all_gather | solution.py:47
  146.9 9.2 %fusion.4 = bf16[512,3584]{1,0:T(8,128)(2,1)} fusion(bf16[512,1024]{1,0:T(8,128)(2,1)} %all-gather.5.cloned.1.call-done, bf16[1,1024,3584]{2,1,0:T(8,128)(2,1)} %param.9), kind=kOutput, calls=%fused_computation.7 | convolution fusion | flops 3759931392 | bytes 12058624 | tf_op jit(solution)/shard_map/dot_general | solution.py:46
  156.0 0.0 copy-start.1
  156.0 7.1 %all-to-all-start.1 = ((bf16[16,32,3584]{2,1,0:T(8,128)(2,1)}), bf16[16,32,3584]{2,1,0:T(8,128)(2,1)}, u32[]{:S(2)}, u32[]{:S(2)}) async-start(bf16[16,32,3584]{2,1,0:T(8,128)(2,1)} %bitcast.32), calls=%async_computation.1 | async-start | bytes 7340032 | tf_op jit(solution)/shard_map/all_to_all | solution.py:51
  163.1 0.0 copy-done.1
  163.1 0.1 copy.18
  163.2 84.2 %all-to-all-done.1 = bf16[16,32,3584]{2,1,0:T(8,128)(2,1)} async-done(((bf16[16,32,3584]{2,1,0:T(8,128)(2,1)}), bf16[16,32,3584]{2,1,0:T(8,128)(2,1)}, u32[]{:S(2)}, u32[]{:S(2)}) %all-to-all-start.1) | async-done | bytes 3670048 | tf_op jit(solution)/shard_map/all_to_all | solution.py:51
  247.5 6.0 %gather_fusion = bf16[256,3584]{1,0:T(8,128)(2,1)S(1)} fusion(bf16[512,3584]{1,0:T(8,128)(2,1)} %bitcast.8, s32[1024]{0:T(1024)S(1)} %pad_clamp_fusion), kind=kCustom, calls=%fused_computation | custom fusion | bytes 3671040 | tf_op jit(solution)/shard_map/gather | solution.py:59
  253.5 0.6 fusion.7
  254.1 0.7 copy.21
  (5 shorter events, 0.0 us)
Async XLA Ops:
  6.5 3.9 %copy-start = (bf16[32,3584]{1,0:T(8,128)(2,1)S(1)}, bf16[32,3584]{1,0:T(8,128)(2,1)}, u32[]{:S(2)}) copy-start(bf16[32,3584]{1,0:T(8,128)(2,1)} %param.5) | copy-start | bytes 688132
  6.5 115.7 %all-gather.3.cloned.1.call-start = ((), (), s32[]{:S(2)}) async-start(), calls=%async_computation.2 | async-start | bytes 11010048 | tf_op jit(solution)/shard_map/all_gather | solution.py:39
  103.6 43.3 %all-gather.5.cloned.1.call-start = ((), (), s32[]{:S(2)}) async-start(), calls=%async_computation.3 | async-start | bytes 1572864 | tf_op jit(solution)/shard_map/all_gather | solution.py:47
  156.0 7.1 %copy-start.1 = (f32[32,8]{0,1:T(8,128)S(1)}, f32[32,8]{0,1:T(8,128)}, u32[]{:S(2)}) copy-start(f32[32,8]{0,1:T(8,128)} %param.7) | copy-start | bytes 3076
  156.0 91.4 %all-to-all-start.1 = ((bf16[16,32,3584]{2,1,0:T(8,128)(2,1)}), bf16[16,32,3584]{2,1,0:T(8,128)(2,1)}, u32[]{:S(2)}, u32[]{:S(2)}) async-start(bf16[16,32,3584]{2,1,0:T(8,128)(2,1)} %bitcast.32), calls=%async_computation.1 | async-start | bytes 7340032 | tf_op jit(solution)/shard_map/all_to_all | solution.py:51
Sparse Core Ops, SparseCore 0:
  103.7 18.5 all-gather.2
  136.6 10.1 all-gather.4
where the time goes:
time: 262 us
  waiting for transfers between devices  113 us (43%)
  blocking collectives  87.7 us (33%)
  matrix products  22.9 us (9%)
  local copies, waits for them, and re-layouts  15.3 us (6%)
  between operations  13.5 us (5%)
  starting transfers between devices  7.13 us (3%)
    all_to_all x1, blocking collectives, per_device(): lax.all_to_all(buffer.reshape(experts, capacity, feat_width), 'expert', s...  87.7 us
    all_to_all x1, waiting for transfers between devices, per_device(): lax.all_to_all(expert_out.reshape(experts, capacity, down_local.shape[1])...  84.2 us
    all_gather x1, waiting for transfers between devices, per_device(): lax.all_gather(token_rows, 'tensor', axis=1, tiled=True)  18.6 us
    dot_general x1, matrix products, per_device(): jnp.dot(lax.all_gather(token_rows, 'tensor', axis=1, tiled=True), weights...  13.1 us
    all_gather x1, waiting for transfers between devices, per_device(): lax.all_gather(hidden, 'tensor', axis=1, tiled=True)  10.4 us
    dot_general x1, matrix products, per_device(): jnp.dot(lax.all_gather(hidden, 'tensor', axis=1, tiled=True), weights, pr...  9.17 us
    all_to_all x1, starting transfers between devices, per_device(): lax.all_to_all(expert_out.reshape(experts, capacity, down_local.shape[1])...  7.09 us
    gather x1, local copies, waits for them, and re-layouts, per_device(): picked = returned_flat[target].reshape(tok_group, TOP, down_local.shape[1])  6.04 us
  transfers between devices with their start and end apart: 3, of which 3 were waited for; matrix products, arithmetic and copies ran while one was open for 0% of the time, Pallas kernels for 0%

commit v1 on v0

v1 whole, which is shorter than its diff:
```python
import functools
import jax
import jax.numpy as jnp
from jax import lax
from jax.experimental import pallas as pl
from jax.experimental.pallas import tpu as pltpu
from jax.sharding import PartitionSpec as P

BF16 = jnp.bfloat16
F32 = jnp.float32


def tile_of(width, most):
    return next(t for t in (most, 256, 128) if width % t == 0)


def line_order(line):
    return sorted(range(1, line), key=lambda d: abs(2 * d - line)) + [0]


def layer_kernel(
    line, tokens, ids, weights, w_in, w_down, out,
    x, w1, w2, acc, hid, y, from_b, to_a, from_a, to_z, from_z,
    w_sem, z_send, a_send, b_send, t_send, x_recv, t_recv, h_send, h_recv,
    rb_send, rb_recv, ra_send, ra_recv, rz_send, rz_recv,
):
    me = lax.axis_index("expert")
    t = lax.axis_index("tensor")
    other = 1 - t
    experts = 4 * line
    rows, feat = tokens.shape
    half = hid.shape[3]
    depth = 2 * feat
    col_x, col_y, col_z = me % 2, (me // 2) % 2, me // 4
    peer_x = me + 1 - 2 * col_x
    peer_y = me + 2 - 4 * col_y
    peer_a = peer_x + t * (peer_y - peer_x)
    peer_b = peer_y + t * (peer_x - peer_y)
    quarter_a, quarter_b = 1 + t, 2 - t

    def peer_z(d):
        return ((col_z + d) % line) * 4 + col_y * 2 + col_x

    w_copies = [
        pltpu.make_async_copy(w_in.at[0, pl.ds(pl.multiple_of(k * feat, 128), feat)],
                              w1.at[pl.ds(pl.multiple_of(k * feat, 128), feat)], w_sem.at[i])
        for i, k in enumerate((t, other))
    ] + [pltpu.make_async_copy(w_down.at[0], w2, w_sem.at[2])]
    for c in w_copies:
        c.start()

    barrier = pltpu.get_barrier_semaphore()
    partners = [(peer_z(d), t) for d in range(1, line)] + [(peer_x, t), (peer_y, t), (me, other)]
    for p in partners:
        pl.semaphore_signal(barrier, inc=1, device_id=p, device_id_type=pl.DeviceIdType.MESH)

    x[t, 0, :, :feat] = tokens[...]
    lane = lax.broadcasted_iota(jnp.int32, (rows, 128), 1)
    table = jnp.zeros((rows, 128), F32)
    for k in range(ids.shape[1]):
        table += jnp.where(lane % experts == ids[:, k:k + 1], weights[:, k:k + 1], 0.0)
    high = table.astype(BF16)
    rest = table - high.astype(F32)
    mid = rest.astype(BF16)
    low = (rest - mid.astype(F32)).astype(BF16)
    part = jnp.where(lane < experts, high.astype(F32),
                     jnp.where(lane < 2 * experts, mid.astype(F32), low.astype(F32)))
    x[t, 0, :, feat:] = jnp.where(lane < 3 * experts, part, 0.0).astype(BF16)

    pl.semaphore_wait(barrier, len(partners))

    def remote(src, dst, send, recv, to):
        return pltpu.make_async_remote_copy(
            src_ref=src, dst_ref=dst, send_sem=send, recv_sem=recv,
            device_id=to, device_id_type=pl.DeviceIdType.MESH)

    def number(db, da, dz):
        return (2 * db + da) * line + dz

    def slot(db, da, dz):
        return (db * quarter_b + da * quarter_a) * line + dz

    def slot_other(db, da, dz):
        return (db * quarter_a + da * quarter_b) * line + dz

    order = line_order(line)
    sent = []

    def send(*args):
        c = remote(*args)
        c.start()
        sent.append(c)

    def forward(db, da, dz):
        src = x.at[t, slot(db, da, dz)]
        if (db, da, dz) == (0, 0, 0):
            for d in order[:-1]:
                send(src, x.at[t, line - d], z_send.at[d - 1], x_recv.at[line - d], (peer_z(d), t))
        if db == 0 and da == 0:
            send(src, x.at[t, slot(0, 1, dz)], a_send.at[dz], x_recv.at[number(0, 1, dz)], (peer_a, t))
        if db == 0:
            send(src, x.at[t, slot(1, da, dz)], b_send.at[number(0, da, dz)],
                 x_recv.at[number(1, da, dz)], (peer_b, t))
        n = number(db, da, dz)
        send(src, src, t_send.at[n], t_recv.at[n], (me, other))

    def arrive(db, da, dz):
        n = number(db, da, dz)
        dst = x.at[t, slot(db, da, dz)]
        remote(dst, dst, t_send.at[n], x_recv.at[n], (me, other)).wait_recv()

    def arrive_other(db, da, dz):
        n = number(db, da, dz)
        dst = x.at[other, slot_other(db, da, dz)]
        remote(dst, dst, t_send.at[n], t_recv.at[n], (me, other)).wait_recv()

    forward(0, 0, 0)
    acc[...] = jnp.zeros_like(acc)
    arrive(0, 1, 0)
    forward(0, 1, 0)
    for d in order[:-1]:
        dz = line - d
        arrive(0, 0, dz)
        forward(0, 0, dz)
        arrive(0, 1, dz)
        forward(0, 1, dz)

    wide = tile_of(2 * half, 256)
    group = line * rows

    def project(tt, q0, q1):
        def step(n, _):
            cols = pl.ds(pl.multiple_of(n * wide, wide), wide)
            block = jnp.concatenate(
                [x[tt, pl.ds(q * line, line), :, :feat].reshape(group, feat) for q in (q0, q1)], axis=0)
            r = jnp.dot(block, w1[pl.ds(pl.multiple_of(tt * feat, 128), feat), cols],
                        preferred_element_type=F32)
            acc[q0, :, cols] += r[:group]
            acc[q1, :, cols] += r[group:]
            return 0

        lax.fori_loop(0, 2 * half // wide, step, 0)

    def hidden(i, q):
        extra = x[t, pl.ds(q * line, line), :, feat:].reshape(group, 128).astype(F32)
        lanes = lax.broadcasted_iota(jnp.int32, (group, 128), 1)
        scale = jnp.sum(jnp.where(lanes % experts == me, extra, 0.0), axis=1, keepdims=True)
        gate = acc[q, :, :half]
        hid[t, q] = (gate / (1.0 + jnp.exp(-gate)) * acc[q, :, half:] * scale).astype(BF16)
        send(hid.at[t, q], hid.at[t, q], h_send.at[i], h_recv.at[i], (me, other))

    def hidden_other(i, q):
        remote(hid.at[other, q], hid.at[other, q], h_send.at[i], h_recv.at[i], (me, other)).wait_recv()

    w_copies[0].wait()
    project(t, 0, quarter_a)
    for dz in range(line):
        for da in range(2):
            arrive_other(0, da, dz)
    w_copies[1].wait()
    project(other, 0, quarter_b)
    hidden(0, 0)
    for dz in [0] + [line - d for d in order[:-1]]:
        for da in range(2):
            arrive(1, da, dz)
            forward(1, da, dz)
    project(t, quarter_b, 3)
    hidden(1, quarter_b)
    for dz in range(line):
        for da in range(2):
            arrive_other(1, da, dz)
    project(other, quarter_a, 3)
    hidden(2, 3)
    hidden(3, quarter_a)

    w_copies[2].wait()
    broad = tile_of(feat, 512)

    def down(q0, q1):
        def step(n, _):
            cols = pl.ds(pl.multiple_of(n * broad, broad), broad)
            block = jnp.concatenate(
                [jnp.concatenate([hid[0, q], hid[1, q]], axis=1) for q in (q0, q1)], axis=0)
            r = jnp.dot(block, w2[:, cols], preferred_element_type=F32).astype(BF16)
            y[pl.ds(q0 * line, line), :, cols] = r[:group].reshape(line, rows, broad)
            y[pl.ds(q1 * line, line), :, cols] = r[group:].reshape(line, rows, broad)
            return 0

        lax.fori_loop(0, feat // broad, step, 0)

    hidden_other(2, 3)
    hidden_other(3, quarter_b)
    down(quarter_b, 3)
    for dz in order:
        for da in (1, 0):
            n = number(0, da, dz)
            send(y.at[slot(1, da, dz)], from_b.at[n], rb_send.at[n], rb_recv.at[n], (peer_b, t))
    hidden_other(0, 0)
    hidden_other(1, quarter_a)
    down(quarter_a, 0)

    def got_b(da, dz):
        n = number(0, da, dz)
        remote(from_b.at[n], from_b.at[n], rb_send.at[n], rb_recv.at[n], (peer_b, t)).wait_recv()

    def got_a(dz):
        remote(from_a.at[dz], from_a.at[dz], ra_send.at[dz], ra_recv.at[dz], (peer_a, t)).wait_recv()

    def pass_a(dz):
        got_b(1, dz)
        to_a[dz] = (y[slot(0, 1, dz)].astype(F32) + from_b[number(0, 1, dz)].astype(F32)).astype(BF16)
        send(to_a.at[dz], from_a.at[dz], ra_send.at[dz], ra_recv.at[dz], (peer_a, t))

    def total(dz):
        got_b(0, dz)
        got_a(dz)
        return y[slot(0, 0, dz)].astype(F32) + from_b[number(0, 0, dz)].astype(F32) + from_a[dz].astype(F32)

    def pass_z(dz):
        to_z[dz - 1] = total(dz).astype(BF16)
        send(to_z.at[dz - 1], from_z.at[dz - 1], rz_send.at[dz - 1], rz_recv.at[dz - 1], (peer_z(dz), t))

    pass_a(order[0])
    for now, later in zip(order, order[1:]):
        pass_a(later)
        pass_z(now)
    result = total(0)
    for d in order[:-1]:
        remote(from_z.at[d - 1], from_z.at[d - 1], rz_send.at[d - 1], rz_recv.at[d - 1],
               (peer_z(d), t)).wait_recv()
        result = result + from_z[d - 1].astype(F32)
    out[...] = result.astype(BF16)
    for c in sent:
        c.wait_send()


def fused(tokens, expert_ids, combine, w_in, w_down):
    line = lax.axis_size("expert") // 4
    rows, feat = tokens.shape
    half = w_in.shape[2] // 2
    dma = pltpu.SemaphoreType.DMA
    block = (rows, feat)
    vmem = pl.BlockSpec(memory_space=pltpu.VMEM)
    hbm = pl.BlockSpec(memory_space=pl.ANY)
    return pl.pallas_call(
        functools.partial(layer_kernel, line),
        out_shape=jax.ShapeDtypeStruct(block, BF16),
        in_specs=[vmem, vmem, vmem, hbm, hbm],
        out_specs=vmem,
        scratch_shapes=[
            pltpu.VMEM((2, 4 * line, rows, feat + 128), BF16),
            pltpu.VMEM(w_in.shape[1:], BF16),
            pltpu.VMEM(w_down.shape[1:], BF16),
            pltpu.VMEM((4, line * rows, 2 * half), F32),
            pltpu.VMEM((2, 4, line * rows, half), BF16),
            pltpu.VMEM((4 * line,) + block, BF16),
            pltpu.VMEM((2 * line,) + block, BF16),
            pltpu.VMEM((line,) + block, BF16),
            pltpu.VMEM((line,) + block, BF16),
            pltpu.VMEM((line - 1,) + block, BF16),
            pltpu.VMEM((line - 1,) + block, BF16),
            dma((3,)), dma((line - 1,)), dma((line,)), dma((2 * line,)), dma((4 * line,)),
            dma((4 * line,)), dma((4 * line,)), dma((4,)), dma((4,)),
            dma((2 * line,)), dma((2 * line,)), dma((line,)), dma((line,)),
            dma((line - 1,)), dma((line - 1,)),
        ],
        compiler_params=pltpu.CompilerParams(
            collective_id=0, has_side_effects=True, vmem_limit_bytes=58 * 1024 * 1024),
    )(tokens, expert_ids, combine, w_in, w_down)


def gathered(tokens, expert_ids, combine, w_in, w_down):
    experts = lax.axis_size("expert")
    me = lax.axis_index("expert")
    named = expert_ids[:, :, None] == jnp.arange(experts, dtype=jnp.int32)[None, None, :]
    table = jnp.sum(jnp.where(named, combine[:, :, None], 0.0), axis=1)
    table = lax.all_gather(table, "expert", axis=0, tiled=True)
    scale = lax.dynamic_slice_in_dim(table, me, 1, axis=1)
    rows = lax.all_gather(tokens, "expert", axis=0, tiled=True)
    rows = lax.all_gather(rows, "tensor", axis=1, tiled=True)
    gate_up = jnp.dot(rows, w_in[0], preferred_element_type=F32)
    half = w_in.shape[2] // 2
    hidden = (jax.nn.silu(gate_up[:, :half]) * gate_up[:, half:]).astype(BF16)
    hidden = lax.all_gather(hidden, "tensor", axis=1, tiled=True)
    out = jnp.dot(hidden, w_down[0], preferred_element_type=F32)
    return lax.psum_scatter((out * scale).astype(BF16), "expert", scatter_dimension=0, tiled=True)


def solution(mesh):
    experts, cores = mesh.shape["expert"], mesh.shape["tensor"]

    def per_device(tokens, expert_ids, combine, w_in, w_down):
        rows, feat = tokens.shape
        fits = (cores == 2 and experts % 4 == 0 and experts >= 8 and 3 * experts <= 128
                and w_in.shape[0] == 1 and rows % 16 == 0 and feat % 128 == 0
                and w_in.shape[2] % 256 == 0)
        run = fused if fits else gathered
        return run(tokens, expert_ids, combine, w_in, w_down)

    in_specs = (
        P("expert", "tensor"),
        P("expert", None),
        P("expert", None),
        P("expert", None, "tensor"),
        P("expert", None, "tensor"),
    )
    return jax.shard_map(
        per_device, mesh=mesh, in_specs=in_specs, out_specs=P("expert", "tensor"), check_vma=False
    )
```

time: 262 us -> 102 us (0.39)
  the two profiles are of different devices: /device:TPU:14 before, /device:TPU:0 now
where the time goes in v1:
time: 102 us
  Pallas kernels  97.3 us (95%)
  local copies, waits for them, and re-layouts  4.37 us (4%)
    pallas_call x1, Pallas kernels, fused(): pl.pallas_call(functools.partial(layer_kernel, line), out_shape=jax.Shape...  97.3 us
    unnamed x3, local copies, waits for them, and re-layouts  4.37 us

profile of v1, /device:TPU:0, one launch (start us, length us, event | category | flops | bytes accessed | tf_op | source)
XLA Modules:
  0.0 101.7 jit_solution(10390599395540001367)
XLA Ops:
  0.0 1.4 %copy.6.ids = s32[32,8]{1,0:T(8,128)} copy(s32[32,8]{0,1:T(8,128)} %param.6) | data formatting | bytes 2048 | tf_op args[1]
  1.4 1.4 %copy.7.weights = f32[32,8]{1,0:T(8,128)} copy(f32[32,8]{0,1:T(8,128)} %param.7) | data formatting | bytes 2048 | tf_op args[2]
  2.7 97.3 %shard_map.55 = bf16[32,3584]{1,0:T(8,128)(2,1)} custom-call(bf16[32,3584]{1,0:T(8,128)(2,1)} %tokens.1, s32[32,8]{1,0:T(8,128)} %copy.6.ids, f32[32,8]{1,0:T(8,128)} %copy.7.weights, bf16[1,7168,1024]{2,1,0:T(8,128)(2,1)} %w_in.1, bf16[1,1024,3584]{2,1,0:T(8,128)(2,1)} %w_down.1), custom_call_target="tpu_custom_call" | custom-call | tf_op jit(solution)/shard_map/pallas_call | solution.py:245
  100.0 1.6 %copy.9 = bf16[32,3584]{1,0:T(8,128)(2,1)} copy(bf16[32,3584]{1,0:T(8,128)(2,1)} %shard_map.55) | data formatting | bytes 458752

commit v2 on v1

--- a/solution.py
+++ b/solution.py
@@ -91,18 +91,45 @@
         c.start()
         sent.append(c)
 
+    def start(*args):
+        remote(*args).start()
+
+    def move_down(dz):
+        return remote(x.at[t, dz], x.at[t, dz + 1], z_send.at[dz], x_recv.at[dz + 1],
+                      (peer_z(line - 1), t))
+
+    def move_up(dz):
+        to = (dz - 1) % line
+        return remote(x.at[t, dz], x.at[t, to], z_send.at[line + dz], x_recv.at[to], (peer_z(1), t))
+
+    def line_moves(do):
+        for dz in range(line - 1):
+            @pl.when((col_z + dz < line) & (col_z > 0))
+            def _():
+                do(move_down(dz))
+        for dz in [0] + list(range(2, line)):
+            @pl.when((col_z + dz >= (line if dz else 0)) & (col_z < line - 1))
+            def _():
+                do(move_up(dz))
+
     def forward(db, da, dz):
         src = x.at[t, slot(db, da, dz)]
-        if (db, da, dz) == (0, 0, 0):
-            for d in order[:-1]:
-                send(src, x.at[t, line - d], z_send.at[d - 1], x_recv.at[line - d], (peer_z(d), t))
         if db == 0 and da == 0:
-            send(src, x.at[t, slot(0, 1, dz)], a_send.at[dz], x_recv.at[number(0, 1, dz)], (peer_a, t))
+            if dz < line - 1:
+                @pl.when((col_z + dz < line) & (col_z > 0))
+                def _():
+                    move_down(dz).start()
+            if dz != 1:
+                @pl.when((col_z + dz >= (line if dz else 0)) & (col_z < line - 1))
+                def _():
+                    move_up(dz).start()
+        if db == 0 and da == 0:
+            start(src, x.at[t, slot(0, 1, dz)], a_send.at[dz], x_recv.at[number(0, 1, dz)], (peer_a, t))
         if db == 0:
-            send(src, x.at[t, slot(1, da, dz)], b_send.at[number(0, da, dz)],
+            start(src, x.at[t, slot(1, da, dz)], b_send.at[number(0, da, dz)],
                  x_recv.at[number(1, da, dz)], (peer_b, t))
         n = number(db, da, dz)
-        send(src, src, t_send.at[n], t_recv.at[n], (me, other))
+        start(src, src, t_send.at[n], t_recv.at[n], (me, other))
 
     def arrive(db, da, dz):
         n = number(db, da, dz)
@@ -114,16 +141,31 @@
         dst = x.at[other, slot_other(db, da, dz)]
         remote(dst, dst, t_send.at[n], t_recv.at[n], (me, other)).wait_recv()
 
+    def at_distance(k, do):
+        if k == 0:
+            do(0)
+            return
+
+        @pl.when(col_z + k < line)
+        def _():
+            do(k)
+
+        @pl.when(col_z >= k)
+        def _():
+            do(line - k)
+
+    def take(db, da):
+        def do(dz):
+            arrive(db, da, dz)
+            forward(db, da, dz)
+        return do
+
     forward(0, 0, 0)
     acc[...] = jnp.zeros_like(acc)
-    arrive(0, 1, 0)
-    forward(0, 1, 0)
-    for d in order[:-1]:
-        dz = line - d
-        arrive(0, 0, dz)
-        forward(0, 0, dz)
-        arrive(0, 1, dz)
-        forward(0, 1, dz)
+    for k in range(1, line + 1):
+        if k < line:
+            at_distance(k, take(0, 0))
+        at_distance(k - 1, take(0, 1))
 
     wide = tile_of(2 * half, 256)
     group = line * rows
@@ -160,10 +202,9 @@
     w_copies[1].wait()
     project(other, 0, quarter_b)
     hidden(0, 0)
-    for dz in [0] + [line - d for d in order[:-1]]:
-        for da in range(2):
-            arrive(1, da, dz)
-            forward(1, da, dz)
+    for k in range(line):
+        at_distance(k, take(1, 0))
+        at_distance(k, take(1, 1))
     project(t, quarter_b, 3)
     hidden(1, quarter_b)
     for dz in range(line):
@@ -232,6 +273,18 @@
     out[...] = result.astype(BF16)
     for c in sent:
         c.wait_send()
+    line_moves(lambda c: c.wait_send())
+    for dz in range(line):
+        for da in range(2):
+            src = x.at[t, slot(0, da, dz)]
+            if da == 0:
+                remote(src, src, a_send.at[dz], x_recv.at[dz], (peer_a, t)).wait_send()
+            n = number(0, da, dz)
+            remote(src, src, b_send.at[n], x_recv.at[n], (peer_b, t)).wait_send()
+            for db in range(2):
+                n = number(db, da, dz)
+                src = x.at[t, slot(db, da, dz)]
+                remote(src, src, t_send.at[n], t_recv.at[n], (me, other)).wait_send()
 
 
 def fused(tokens, expert_ids, combine, w_in, w_down):
@@ -259,7 +312,7 @@
             pltpu.VMEM((line,) + block, BF16),
             pltpu.VMEM((line - 1,) + block, BF16),
             pltpu.VMEM((line - 1,) + block, BF16),
-            dma((3,)), dma((line - 1,)), dma((line,)), dma((2 * line,)), dma((4 * line,)),
+            dma((3,)), dma((2 * line,)), dma((line,)), dma((2 * line,)), dma((4 * line,)),
             dma((4 * line,)), dma((4 * line,)), dma((4,)), dma((4,)),
             dma((2 * line,)), dma((2 * line,)), dma((line,)), dma((line,)),
             dma((line - 1,)), dma((line - 1,)),

time: 102 us -> 89.6 us (0.88)
  Pallas kernels: 97.3 us -> 85 us
    pallas_call x1, Pallas kernels: 97.3 us -> 85 us  [fused(): pl.pallas_call(functools.partial(layer_kernel, line), out_shape=jax.Shape...]
where the time goes in v2:
time: 89.6 us; the launch traced here: 89.4 us
  Pallas kernels  85 us (95%)
  local copies, waits for them, and re-layouts  4.37 us (5%)
    pallas_call x1, Pallas kernels, fused(): pl.pallas_call(functools.partial(layer_kernel, line), out_shape=jax.Shape...  85 us
    unnamed x3, local copies, waits for them, and re-layouts  4.37 us

profile of v2, /device:TPU:0, one launch (start us, length us, event | category | flops | bytes accessed | tf_op | source)
XLA Modules:
  0.0 89.4 jit_solution(8013783655115332081)
XLA Ops:
  0.0 1.4 %copy.6.ids = s32[32,8]{1,0:T(8,128)} copy(s32[32,8]{0,1:T(8,128)} %param.6) | data formatting | bytes 2048 | tf_op args[1]
  1.4 1.4 %copy.7.weights = f32[32,8]{1,0:T(8,128)} copy(f32[32,8]{0,1:T(8,128)} %param.7) | data formatting | bytes 2048 | tf_op args[2]
  2.7 85.0 %shard_map.55 = bf16[32,3584]{1,0:T(8,128)(2,1)} custom-call(bf16[32,3584]{1,0:T(8,128)(2,1)} %tokens.1, s32[32,8]{1,0:T(8,128)} %copy.6.ids, f32[32,8]{1,0:T(8,128)} %copy.7.weights, bf16[1,7168,1024]{2,1,0:T(8,128)(2,1)} %w_in.1, bf16[1,1024,3584]{2,1,0:T(8,128)(2,1)} %w_down.1), custom_call_target="tpu_custom_call" | custom-call | tf_op jit(solution)/shard_map/pallas_call | solution.py:298
  87.8 1.6 %copy.9 = bf16[32,3584]{1,0:T(8,128)(2,1)} copy(bf16[32,3584]{1,0:T(8,128)(2,1)} %shard_map.55) | data formatting | bytes 458752

commit v3 on v1

--- a/solution.py
+++ b/solution.py
@@ -19,7 +19,7 @@
 
 
 def layer_kernel(
-    line, tokens, ids, weights, w_in, w_down, out,
+    line, parts, tokens, routes, w_in, w_down, out,
     x, w1, w2, acc, hid, y, from_b, to_a, from_a, to_z, from_z,
     w_sem, z_send, a_send, b_send, t_send, x_recv, t_recv, h_send, h_recv,
     rb_send, rb_recv, ra_send, ra_recv, rz_send, rz_recv,
@@ -29,6 +29,7 @@
     other = 1 - t
     experts = 4 * line
     rows, feat = tokens.shape
+    piece = rows // parts
     half = hid.shape[3]
     depth = 2 * feat
     col_x, col_y, col_z = me % 2, (me // 2) % 2, me // 4
@@ -56,9 +57,11 @@
 
     x[t, 0, :, :feat] = tokens[...]
     lane = lax.broadcasted_iota(jnp.int32, (rows, 128), 1)
+    expert_of = (lane % experts).astype(F32)
+    top = routes.shape[1] // 2
     table = jnp.zeros((rows, 128), F32)
-    for k in range(ids.shape[1]):
-        table += jnp.where(lane % experts == ids[:, k:k + 1], weights[:, k:k + 1], 0.0)
+    for k in range(top):
+        table += jnp.where(expert_of == routes[:, k:k + 1], routes[:, top + k:top + k + 1], 0.0)
     high = table.astype(BF16)
     rest = table - high.astype(F32)
     mid = rest.astype(BF16)
@@ -91,39 +94,82 @@
         c.start()
         sent.append(c)
 
-    def forward(db, da, dz):
-        src = x.at[t, slot(db, da, dz)]
-        if (db, da, dz) == (0, 0, 0):
-            for d in order[:-1]:
-                send(src, x.at[t, line - d], z_send.at[d - 1], x_recv.at[line - d], (peer_z(d), t))
+    def rows_of(h):
+        return pl.ds(h * piece, piece)
+
+    def own(db, da, dz, h):
+        return x.at[t, slot(db, da, dz), rows_of(h)]
+
+    def move_down(dz, h):
+        return remote(x.at[t, dz, rows_of(h)], x.at[t, dz + 1, rows_of(h)], z_send.at[dz, h],
+                      x_recv.at[dz + 1, h], (peer_z(line - 1), t))
+
+    def move_up(dz, h):
+        to = (dz - 1) % line
+        return remote(x.at[t, dz, rows_of(h)], x.at[t, to, rows_of(h)], z_send.at[line + dz, h],
+                      x_recv.at[to, h], (peer_z(1), t))
+
+    def line_moves(dz, h, do):
+        if dz < line - 1:
+            @pl.when((col_z + dz < line) & (col_z > 0))
+            def _():
+                do(move_down(dz, h))
+        if dz != 1:
+            @pl.when((col_z + dz >= (line if dz else 0)) & (col_z < line - 1))
+            def _():
+                do(move_up(dz, h))
+
+    def moves(db, da, dz, h, do):
+        src = own(db, da, dz, h)
+        n = number(db, da, dz)
         if db == 0 and da == 0:
-            send(src, x.at[t, slot(0, 1, dz)], a_send.at[dz], x_recv.at[number(0, 1, dz)], (peer_a, t))
+            line_moves(dz, h, do)
+            do(remote(src, own(0, 1, dz, h), a_send.at[dz, h], x_recv.at[number(0, 1, dz), h], (peer_a, t)))
         if db == 0:
-            send(src, x.at[t, slot(1, da, dz)], b_send.at[number(0, da, dz)],
-                 x_recv.at[number(1, da, dz)], (peer_b, t))
+            do(remote(src, own(1, da, dz, h), b_send.at[n, h], x_recv.at[number(1, da, dz), h], (peer_b, t)))
+        do(remote(src, src, t_send.at[n, h], t_recv.at[n, h], (me, other)))
+
+    def forward(db, da, dz, h):
+        moves(db, da, dz, h, lambda c: c.start())
+
+    def arrive(db, da, dz, h):
         n = number(db, da, dz)
-        send(src, src, t_send.at[n], t_recv.at[n], (me, other))
-
-    def arrive(db, da, dz):
-        n = number(db, da, dz)
-        dst = x.at[t, slot(db, da, dz)]
-        remote(dst, dst, t_send.at[n], x_recv.at[n], (me, other)).wait_recv()
+        dst = own(db, da, dz, h)
+        remote(dst, dst, t_send.at[n, h], x_recv.at[n, h], (me, other)).wait_recv()
 
     def arrive_other(db, da, dz):
         n = number(db, da, dz)
-        dst = x.at[other, slot_other(db, da, dz)]
-        remote(dst, dst, t_send.at[n], t_recv.at[n], (me, other)).wait_recv()
-
-    forward(0, 0, 0)
+        for h in range(parts):
+            dst = x.at[other, slot_other(db, da, dz), rows_of(h)]
+            remote(dst, dst, t_send.at[n, h], t_recv.at[n, h], (me, other)).wait_recv()
+
+    def at_distance(k, do):
+        if k == 0:
+            do(0)
+            return
+
+        @pl.when(col_z + k < line)
+        def _():
+            do(k)
+
+        @pl.when(col_z >= k)
+        def _():
+            do(line - k)
+
+    def take(db, da, h):
+        def do(dz):
+            arrive(db, da, dz, h)
+            forward(db, da, dz, h)
+        return do
+
+    for h in range(parts):
+        forward(0, 0, 0, h)
     acc[...] = jnp.zeros_like(acc)
-    arrive(0, 1, 0)
-    forward(0, 1, 0)
-    for d in order[:-1]:
-        dz = line - d
-        arrive(0, 0, dz)
-        forward(0, 0, dz)
-        arrive(0, 1, dz)
-        forward(0, 1, dz)
+    for k in range(1, line + 1):
+        for h in range(parts):
+            if k < line:
+                at_distance(k, take(0, 0, h))
+            at_distance(k - 1, take(0, 1, h))
 
     wide = tile_of(2 * half, 256)
     group = line * rows
@@ -160,10 +206,10 @@
     w_copies[1].wait()
     project(other, 0, quarter_b)
     hidden(0, 0)
-    for dz in [0] + [line - d for d in order[:-1]]:
-        for da in range(2):
-            arrive(1, da, dz)
-            forward(1, da, dz)
+    for k in range(line):
+        for h in range(parts):
+            at_distance(k, take(1, 0, h))
+            at_distance(k, take(1, 1, h))
     project(t, quarter_b, 3)
     hidden(1, quarter_b)
     for dz in range(line):
@@ -194,58 +240,71 @@
     for dz in order:
         for da in (1, 0):
             n = number(0, da, dz)
-            send(y.at[slot(1, da, dz)], from_b.at[n], rb_send.at[n], rb_recv.at[n], (peer_b, t))
+            for h in range(parts):
+                send(y.at[slot(1, da, dz), rows_of(h)], from_b.at[n, rows_of(h)],
+                     rb_send.at[n, h], rb_recv.at[n, h], (peer_b, t))
     hidden_other(0, 0)
     hidden_other(1, quarter_a)
     down(quarter_a, 0)
 
-    def got_b(da, dz):
-        n = number(0, da, dz)
-        remote(from_b.at[n], from_b.at[n], rb_send.at[n], rb_recv.at[n], (peer_b, t)).wait_recv()
-
-    def got_a(dz):
-        remote(from_a.at[dz], from_a.at[dz], ra_send.at[dz], ra_recv.at[dz], (peer_a, t)).wait_recv()
-
-    def pass_a(dz):
-        got_b(1, dz)
-        to_a[dz] = (y[slot(0, 1, dz)].astype(F32) + from_b[number(0, 1, dz)].astype(F32)).astype(BF16)
-        send(to_a.at[dz], from_a.at[dz], ra_send.at[dz], ra_recv.at[dz], (peer_a, t))
-
-    def total(dz):
-        got_b(0, dz)
-        got_a(dz)
-        return y[slot(0, 0, dz)].astype(F32) + from_b[number(0, 0, dz)].astype(F32) + from_a[dz].astype(F32)
-
-    def pass_z(dz):
-        to_z[dz - 1] = total(dz).astype(BF16)
-        send(to_z.at[dz - 1], from_z.at[dz - 1], rz_send.at[dz - 1], rz_recv.at[dz - 1], (peer_z(dz), t))
-
-    pass_a(order[0])
+    def got(buf, send_sem, recv_sem, n, h, to):
+        ref = buf.at[n, rows_of(h)]
+        remote(ref, ref, send_sem.at[n, h], recv_sem.at[n, h], to).wait_recv()
+
+    def pass_a(dz, h):
+        n = number(0, 1, dz)
+        got(from_b, rb_send, rb_recv, n, h, (peer_b, t))
+        r = rows_of(h)
+        to_a[dz, r] = (y[slot(0, 1, dz), r].astype(F32) + from_b[n, r].astype(F32)).astype(BF16)
+        send(to_a.at[dz, r], from_a.at[dz, r], ra_send.at[dz, h], ra_recv.at[dz, h], (peer_a, t))
+
+    def total(dz, h):
+        got(from_b, rb_send, rb_recv, dz, h, (peer_b, t))
+        got(from_a, ra_send, ra_recv, dz, h, (peer_a, t))
+        r = rows_of(h)
+        return y[slot(0, 0, dz), r].astype(F32) + from_b[dz, r].astype(F32) + from_a[dz, r].astype(F32)
+
+    def pass_z(dz, h):
+        r = rows_of(h)
+        to_z[dz - 1, r] = total(dz, h).astype(BF16)
+        send(to_z.at[dz - 1, r], from_z.at[dz - 1, r], rz_send.at[dz - 1, h], rz_recv.at[dz - 1, h],
+             (peer_z(dz), t))
+
+    for h in range(parts):
+        pass_a(order[0], h)
     for now, later in zip(order, order[1:]):
-        pass_a(later)
-        pass_z(now)
-    result = total(0)
-    for d in order[:-1]:
-        remote(from_z.at[d - 1], from_z.at[d - 1], rz_send.at[d - 1], rz_recv.at[d - 1],
-               (peer_z(d), t)).wait_recv()
-        result = result + from_z[d - 1].astype(F32)
-    out[...] = result.astype(BF16)
+        for h in range(parts):
+            pass_a(later, h)
+            pass_z(now, h)
+    for h in range(parts):
+        result = total(0, h)
+        for d in order[:-1]:
+            got(from_z, rz_send, rz_recv, d - 1, h, (peer_z(d), t))
+            result = result + from_z[d - 1, rows_of(h)].astype(F32)
+        out[rows_of(h)] = result.astype(BF16)
     for c in sent:
         c.wait_send()
+    for db in range(2):
+        for da in range(2):
+            for dz in range(line):
+                for h in range(parts):
+                    moves(db, da, dz, h, lambda c: c.wait_send())
 
 
 def fused(tokens, expert_ids, combine, w_in, w_down):
     line = lax.axis_size("expert") // 4
     rows, feat = tokens.shape
     half = w_in.shape[2] // 2
+    routes = jnp.concatenate([expert_ids.astype(F32), combine], axis=1)
+    parts = 2 if rows % 32 == 0 else 1
     dma = pltpu.SemaphoreType.DMA
     block = (rows, feat)
     vmem = pl.BlockSpec(memory_space=pltpu.VMEM)
     hbm = pl.BlockSpec(memory_space=pl.ANY)
     return pl.pallas_call(
-        functools.partial(layer_kernel, line),
+        functools.partial(layer_kernel, line, parts),
         out_shape=jax.ShapeDtypeStruct(block, BF16),
-        in_specs=[vmem, vmem, vmem, hbm, hbm],
+        in_specs=[vmem, vmem, hbm, hbm],
         out_specs=vmem,
         scratch_shapes=[
             pltpu.VMEM((2, 4 * line, rows, feat + 128), BF16),
@@ -259,14 +318,14 @@
             pltpu.VMEM((line,) + block, BF16),
             pltpu.VMEM((line - 1,) + block, BF16),
             pltpu.VMEM((line - 1,) + block, BF16),
-            dma((3,)), dma((line - 1,)), dma((line,)), dma((2 * line,)), dma((4 * line,)),
-            dma((4 * line,)), dma((4 * line,)), dma((4,)), dma((4,)),
-            dma((2 * line,)), dma((2 * line,)), dma((line,)), dma((line,)),
-            dma((line - 1,)), dma((line - 1,)),
+            dma((3,)), dma((2 * line, parts)), dma((line, parts)), dma((2 * line, parts)),
+            dma((4 * line, parts)), dma((4 * line, parts)), dma((4 * line, parts)), dma((4,)), dma((4,)),
+            dma((2 * line, parts)), dma((2 * line, parts)), dma((line, parts)), dma((line, parts)),
+            dma((line - 1, parts)), dma((line - 1, parts)),
         ],
         compiler_params=pltpu.CompilerParams(
             collective_id=0, has_side_effects=True, vmem_limit_bytes=58 * 1024 * 1024),
-    )(tokens, expert_ids, combine, w_in, w_down)
+    )(tokens, routes, w_in, w_down)
 
 
 def gathered(tokens, expert_ids, combine, w_in, w_down):

time: 102 us -> 87.7 us (0.86)
  Pallas kernels: 97.3 us -> 83.6 us
  local copies, waits for them, and re-layouts: 4.37 us -> 2.48 us
  other arithmetic: 0 us -> 1.37 us
    pallas_call x1, Pallas kernels: 97.3 us -> 83.6 us  [fused(): pl.pallas_call(functools.partial(layer_kernel, line, parts), out_shape=ja...]
    unnamed x3 -> x2, local copies, waits for them, and re-layouts: 4.37 us -> 2.4 us
where the time goes in v3:
time: 87.7 us; the launch traced here: 87.4 us
  Pallas kernels  83.6 us (95%)
  local copies, waits for them, and re-layouts  2.48 us (3%)
  other arithmetic  1.37 us (2%)
    pallas_call x1, Pallas kernels, fused(): pl.pallas_call(functools.partial(layer_kernel, line, parts), out_shape=ja...  83.6 us
    unnamed x2, local copies, waits for them, and re-layouts  2.4 us

profile of v3, /device:TPU:0, one launch (start us, length us, event | category | flops | bytes accessed | tf_op | source)
XLA Modules:
  0.0 87.4 jit_solution(10741591186253781430)
XLA Ops:
  0.0 0.7 convert_element_type.3
  0.7 0.1 copy.8
  0.8 0.8 copy.9
  1.5 0.7 pad_maximum_fusion.routes
  2.2 83.6 %shard_map.55 = bf16[32,3584]{1,0:T(8,128)(2,1)} custom-call(bf16[32,3584]{1,0:T(8,128)(2,1)} %tokens.1, f32[32,16]{1,0:T(8,128)} %pad_maximum_fusion.routes, bf16[1,7168,1024]{2,1,0:T(8,128)(2,1)} %w_in.1, bf16[1,1024,3584]{2,1,0:T(8,128)(2,1)} %w_down.1), custom_call_target="tpu_custom_call" | custom-call | tf_op jit(solution)/shard_map/pallas_call | solution.py:304
  85.8 1.6 %copy.11 = bf16[32,3584]{1,0:T(8,128)(2,1)} copy(bf16[32,3584]{1,0:T(8,128)(2,1)} %shard_map.55) | data formatting | bytes 458752
